TPU v7x, 32 devices: a whole 2x2x4 slice. The times are simulated.
32 devices in a mesh: groups: 2 (over x), expert: 4 (over y, core), tensor: 4 (over z).
Axes of the slice: x: 2, y: 2, z: 4, core: 2. Of those that a mesh axis runs over, the one named last changes fastest.
Arguments:
- tokens: bfloat16 [512, 2880], P(('groups', 'expert', 'tensor')), parts along dimension 0, may hold values from -6 to 6
- routes: int32 [512, 4], P(('groups', 'expert', 'tensor')), parts along dimension 0, may hold values from 0 to 15, all different within a row; in each aligned block of 16 rows (0 to 15, 16 to 31, ...) at most 8 rows name the same one
- route_weights: float32 [512, 4], P(('groups', 'expert', 'tensor')), parts along dimension 0, may hold values from 0.05 to 0.7
- w_gate_up: bfloat16 [16, 2880, 2, 2880], P('expert', None, None, 'tensor'), may hold values from -0.109375 to 0.109375
- bias_gate_up: float32 [16, 2, 2880], P('expert', None, 'tensor'), may hold values from -3 to 3
- w_down: bfloat16 [16, 2880, 2880], P('expert', 'tensor'), may hold values from -0.109375 to 0.109375
- down_bias: float32 [16, 2880], replicated, may hold values from -3 to 3
Outputs:
- moe_output: bfloat16 [512, 2880], P(('groups', 'expert', 'tensor')), parts along dimension 0
There are 2 independent parts, one for each index of `groups`. A program takes and returns all parts, laid end to end along the dimension named above; an argument that names none is the same for every part. Nothing has to cross between parts.
Inputs may be any that keep to these rules, and one draw needn't show every extreme that they name: `routes`: each row names 4 different experts. In each aligned block of 16 rows (the rows of one device) no expert is named more than 8 times, a bound that some block reaches.
All inputs are finite; a program needn't handle non-finite values.
Results may differ from a plain program's by a relative error of at most 0.014.
Values may be sent and summed in bfloat16 or wider, within the bound.
A program may use at most 128 MiB of HBM per device.

v0:
```python
import jax
import jax.numpy as jnp
from jax import lax
from jax.sharding import PartitionSpec as P

TOP = 4
EXPERTS = 16
CAP = 8


def activate(projected, half_width):
    gate_part = projected[..., :half_width]
    up_part = projected[..., half_width:]
    return (gate_part * jax.nn.sigmoid(1.702 * gate_part) * (up_part + 1.0)).astype(jnp.bfloat16)


def local(tokens, routes, route_weights, w_gate_up, bias_gate_up, w_down, down_bias):
    tok_rows, model_width = tokens.shape
    n_expert = lax.axis_size("expert")
    local_count = EXPERTS // n_expert
    slot_total = EXPERTS * CAP
    half_width = w_gate_up.shape[3]
    flat_routes = routes.reshape(-1)
    hit_table = (flat_routes[:, None] == jnp.arange(EXPERTS, dtype=jnp.int32)[None, :]).astype(
        jnp.int32
    )
    before = jnp.cumsum(hit_table, axis=0) - hit_table
    slot = jnp.sum(before * hit_table, axis=1)
    target = (flat_routes * CAP + slot).reshape(tok_rows, TOP)
    choose = target[:, :, None] == jnp.arange(slot_total, dtype=jnp.int32)[None, None, :]
    pick_table = jnp.sum(choose, axis=1).astype(jnp.bfloat16)
    outgoing = jnp.einsum("ts,td->sd", pick_table, tokens, preferred_element_type=jnp.float32)
    outgoing = outgoing.astype(jnp.bfloat16).reshape(n_expert, local_count, CAP, model_width)
    w_joined = w_gate_up.reshape(local_count, model_width, 2 * half_width)
    bias_joined = bias_gate_up.reshape(local_count, 2 * half_width)
    received = lax.all_to_all(outgoing, "expert", split_axis=0, concat_axis=0, tiled=True)
    projected = jnp.einsum(
        "...lcd,ldf->...lcf",
        lax.all_gather(received, "tensor", axis=0, tiled=True),
        w_joined,
        preferred_element_type=jnp.float32,
    )
    hidden = activate(projected + bias_joined[:, None, :], half_width)
    summed = lax.psum_scatter(
        jnp.einsum("rlcf,lfd->rlcd", hidden, w_down, preferred_element_type=jnp.float32).astype(
            jnp.bfloat16
        ),
        "tensor",
        scatter_dimension=0,
        tiled=True,
    ).astype(jnp.float32)
    own_bias = lax.dynamic_slice_in_dim(
        down_bias, lax.axis_index("expert") * local_count, local_count, 0
    )
    result = (summed + own_bias[None, :, None, :]).astype(jnp.bfloat16)
    back = lax.all_to_all(result, "expert", split_axis=0, concat_axis=0, tiled=True)
    slot_table = back.reshape(slot_total, model_width).astype(jnp.float32)
    weighted = jnp.sum(route_weights[:, :, None] * choose.astype(jnp.float32), axis=1)
    combined = jnp.dot(weighted, slot_table, precision=lax.Precision.HIGHEST)
    return combined.astype(jnp.bfloat16)


def solution(mesh):
    return jax.shard_map(
        local,
        mesh=mesh,
        in_specs=(
            P(("groups", "expert", "tensor"), None),
            P(("groups", "expert", "tensor"), None),
            P(("groups", "expert", "tensor"), None),
            P("expert", None, None, "tensor"),
            P("expert", None, "tensor"),
            P("expert", "tensor", None),
            P(),
        ),
        out_specs=P(("groups", "expert", "tensor"), None),
        check_vma=False,
    )
```

profile of v0, /device:TPU:0, one launch (start us, length us, event | category | flops | bytes accessed | tf_op | source)
XLA Modules:
  0.0 257.0 jit_solution(8698965249266490324)
XLA Ops:
  6.5 0.0 copy-start
  6.5 0.0 all-gather.2.cloned.1.call-start
  6.5 0.8 copy.30
  7.3 0.1 eq.28
  7.4 0.1 fusion.14
  7.5 0.1 reduce_window_sum.11
  7.6 0.2 select_reduce_fusion.1
  7.8 0.1 reduce_sum.30
  7.9 0.1 copy.31
  8.0 0.7 multiply_add_fusion
  8.7 0.1 convert_reduce_fusion
  8.7 1.3 convolution_convert_fusion
  10.1 0.4 copy.32
  10.4 15.3 %all_to_all.10 = bf16[4,4,8,2880]{3,2,1,0:T(8,128)(2,1)S(1)} all-to-all(bf16[4,4,8,2880]{3,2,1,0:T(8,128)(2,1)S(1)} %bitcast.32), channel_id=1, replica_groups=mesh['groups'=2,'expert'=4,'tensor'=4] {'expert'}, dimensions={0} | all-to-all | bytes 1474560 | tf_op jit(solution)/shard_map/all_to_all | solution.py:36
  25.8 0.9 copy.33
  26.7 0.0 all-gather.2.cloned.1.call-update
  26.7 0.0 all-reduce.3.cloned.1.call-start
  26.8 0.1 add.38
  26.9 61.6 %all-gather.2.cloned.1.call-done = bf16[16,4,8,2880]{3,2,0,1:T(8,128)(2,1)} async-done(((bf16[4,4,8,2880]{3,2,0,1:T(8,128)(2,1)}), bf16[16,4,8,2880]{3,2,0,1:T(8,128)(2,1)}) %all-gather.2.cloned.1.call-update) | async-done | bytes 2949136 | tf_op jit(solution)/shard_map/all_gather | solution.py:39
  88.5 17.5 %fusion.8 = f32[16,4,8,1440]{3,2,0,1:T(8,128)S(1)} fusion(bf16[16,4,8,2880]{3,2,0,1:T(8,128)(2,1)} %all-gather.2.cloned.1.call-done, bf16[4,2880,1440,1]{1,2,3,0:T(8,128)(2,1)} %bitcast.30, f32[4,1440]{1,0:T(4,128)S(1)} %add.38), kind=kOutput, calls=%fused_computation.7 | convolution fusion | flops 4247470080 | bytes 39098880 | tf_op jit(solution)/shard_map/...lcd,ldf->...lcf/dot_general | solution.py:37
  106.0 10.4 %fusion.5 = bf16[16,4,8,2880]{3,2,0,1:T(8,128)(2,1)} fusion(bf16[4,720,2880]{2,1,0:T(8,128)(2,1)} %param.12, f32[16,4,8,1440]{3,2,0,1:T(8,128)S(1)} %fusion.8), kind=kOutput, calls=%fused_computation.3 | convolution fusion | flops 2127790080 | bytes 22487040 | tf_op jit(solution)/shard_map/rlcf,lfd->rlcd/dot_general | solution.py:45
  116.4 0.0 all-reduce.3.cloned.1.call-update
  116.4 0.0 copy-start.2
  116.4 0.6 copy-done.3
  117.1 0.6 dynamic-slice
  118.3 113.8 %all-reduce.3.cloned.1.call-done = bf16[16,4,8,2880]{3,2,0,1:T(8,128)(2,1)} async-done(((bf16[16,4,8,2880]{3,2,0,1:T(8,128)(2,1)}), bf16[16,4,8,2880]{3,2,0,1:T(8,128)(2,1)}) %all-reduce.3.cloned.1.call-update) | async-done | bytes 2949136
  232.1 1.2 add_convert_fusion
  233.4 0.9 copy.34
  234.3 3.5 %all-to-all-start.1 = ((bf16[4,4,8,2880]{3,2,1,0:T(8,128)(2,1)}), bf16[4,4,8,2880]{3,2,1,0:T(8,128)(2,1)S(1)}, u32[]{:S(2)}, u32[]{:S(2)}) async-start(bf16[4,4,8,2880]{3,2,1,0:T(8,128)(2,1)} %copy.34), calls=%async_computation.1 | async-start | bytes 1507328 | tf_op jit(solution)/shard_map/all_to_all | solution.py:56
  237.8 0.1 select_reduce_fusion
  237.9 11.2 %all-to-all-done.1 = bf16[4,4,8,2880]{3,2,1,0:T(8,128)(2,1)S(1)} async-done(((bf16[4,4,8,2880]{3,2,1,0:T(8,128)(2,1)}), bf16[4,4,8,2880]{3,2,1,0:T(8,128)(2,1)S(1)}, u32[]{:S(2)}, u32[]{:S(2)}) %all-to-all-start.1) | async-done | bytes 737312 | tf_op jit(solution)/shard_map/all_to_all | solution.py:56
  249.1 1.1 convolution_convert_fusion.1
  (6 shorter events, 0.0 us)
Async XLA Ops:
  6.5 111.8 %copy-start = (f32[16,2880]{1,0:T(8,128)S(1)}, f32[16,2880]{1,0:T(8,128)}, u32[]{:S(2)}) copy-start(f32[16,2880]{1,0:T(8,128)} %param.13) | copy-start | bytes 552964
  6.5 81.9 %all-gather.2.cloned.1.call-start = ((), (), s32[]{:S(2)}) async-start(), calls=%async_computation.2 | async-start | bytes 3768320 | tf_op jit(solution)/shard_map/all_gather | solution.py:39
  8.7 18.0 %copy-start.1 = (f32[4,2,720]{2,1,0:T(2,128)S(1)}, f32[4,2,720]{2,1,0:T(2,128)}, u32[]{:S(2)}) copy-start(f32[4,2,720]{2,1,0:T(2,128)} %param.11) | copy-start | bytes 69124
  26.7 205.4 %all-reduce.3.cloned.1.call-start = ((), (), s32[]{:S(2)}) async-start(), calls=%async_computation.3 | async-start | bytes 6029312
  116.4 0.7 copy-start.3
  116.4 121.4 %copy-start.2 = (f32[16,4]{0,1:T(4,128)S(1)}, f32[16,4]{0,1:T(4,128)}, u32[]{:S(2)}) copy-start(f32[16,4]{0,1:T(4,128)} %param.9) | copy-start | bytes 772
  234.3 14.8 %all-to-all-start.1 = ((bf16[4,4,8,2880]{3,2,1,0:T(8,128)(2,1)}), bf16[4,4,8,2880]{3,2,1,0:T(8,128)(2,1)S(1)}, u32[]{:S(2)}, u32[]{:S(2)}) async-start(bf16[4,4,8,2880]{3,2,1,0:T(8,128)(2,1)} %copy.34), calls=%async_computation.1 | async-start | bytes 1507328 | tf_op jit(solution)/shard_map/all_to_all | solution.py:56
Sparse Core Ops, SparseCore 0:
  26.8 61.5 all-gather.1
  116.5 115.5 all-reduce.2
where the time goes:
time: 257 us
  waiting for transfers between devices  187 us (73%)
  matrix products  30.3 us (12%)
  blocking collectives  15.3 us (6%)
  between operations  14.2 us (6%)
  local copies, waits for them, and re-layouts  4.58 us (2%)
  starting transfers between devices  3.53 us (1%)
    unnamed x3, waiting for transfers between devices  114 us
    all_gather x1, waiting for transfers between devices, local(): lax.all_gather(received, 'tensor', axis=0, tiled=True)  61.6 us
    dot_general x1, matrix products, local(): jnp.einsum('...lcd,ldf->...lcf', lax.all_gather(received, 'tensor', axis=...  17.5 us
    all_to_all x1, blocking collectives, local(): lax.all_to_all(outgoing, 'expert', split_axis=0, concat_axis=0, tiled=True)  15.3 us
    all_to_all x1, waiting for transfers between devices, local(): lax.all_to_all(result, 'expert', split_axis=0, concat_axis=0, tiled=True)  11.2 us
    dot_general x1, matrix products, local(): jnp.einsum('rlcf,lfd->rlcd', hidden, w_down, preferred_element_type=jnp.f...  10.4 us
  transfers between devices with their start and end apart: 3, of which 3 were waited for; matrix products, arithmetic and copies ran while one was open for 0% of the time, Pallas kernels for 0%

commit v1 on v0

--- a/solution.py
+++ b/solution.py
@@ -1,6 +1,10 @@
+import functools
+
 import jax
 import jax.numpy as jnp
 from jax import lax
+from jax.experimental import pallas as pl
+from jax.experimental.pallas import tpu as pltpu
 from jax.sharding import PartitionSpec as P
 
 TOP = 4
@@ -60,9 +64,252 @@
     return combined.astype(jnp.bfloat16)
 
 
+MESH = pl.DeviceIdType.MESH
+
+
+def fused(widths, tok_ref, route_ref, weight_ref, bias_ref, down_bias_ref, wg_hbm, wd_hbm, out_ref, *scratch):
+    (wg, wd, xs, xt, ht, hid, bias_t, keep, base, ag_send, ag_recv, rs_send, rs_recv, w_sem) = scratch[:14]
+    chunks = len(widths)
+    send1, recv1, send2, recv2, send3, recv3 = (
+        scratch[14 + i * chunks : 14 + (i + 1) * chunks] for i in range(6)
+    )
+    count, _, half_width, model = wg_hbm.shape
+    rows = tok_ref.shape[0]
+    g, e, t = lax.axis_index("groups"), lax.axis_index("expert"), lax.axis_index("tensor")
+    core_peer = (g, e + 1 - 2 * (e % 2), t)
+    y_peer = (g, (e + 2) % 4, t)
+    z_peers = (
+        None,
+        (g, e, t + 1 - 2 * (t % 2)),
+        (g, e, (t + 2) % 4),
+        (g, e, 3 - t),
+    )
+    partners = (core_peer, y_peer, z_peers[1], z_peers[2], z_peers[3])
+
+    barrier = pltpu.get_barrier_semaphore()
+    for partner in partners:
+        pl.semaphore_signal(barrier, inc=1, device_id=partner, device_id_type=MESH)
+
+    loads = []
+    for l in range(count):
+        loads.append(pltpu.make_async_copy(wg_hbm.at[l], wg.at[l], w_sem.at[l]))
+    for l in range(count):
+        loads.append(
+            pltpu.make_async_copy(
+                wd_hbm.at[l], wd.at[pl.ds(l * half_width, half_width)], w_sem.at[count + l]
+            )
+        )
+    for load in loads:
+        load.start()
+
+    expert_at = lax.broadcasted_iota(jnp.int32, (128, rows), 0)
+    table_t = jnp.zeros((128, rows), jnp.float32)
+    for k in range(TOP):
+        table_t += jnp.where(
+            expert_at % EXPERTS == route_ref[k : k + 1, :], weight_ref[k : k + 1, :], 0.0
+        )
+    table = jnp.transpose(
+        jnp.concatenate([table_t, jnp.zeros((128, 128 - rows), jnp.float32)], axis=1)
+    )[:rows]
+    high = table.astype(jnp.bfloat16).astype(jnp.float32)
+    lane = lax.broadcasted_iota(jnp.int32, (rows, 128), 1)
+    coded = jnp.where(lane < EXPERTS, high, jnp.where(lane < 2 * EXPERTS, table - high, 0.0))
+    wide = xs.shape[2]
+    xs[0, :, :model] = tok_ref[...]
+    xs[0, :, wide - 128 :] = coded.astype(jnp.bfloat16)
+
+    pl.semaphore_wait(barrier, len(partners))
+
+    def hop(index, source, target, peer):
+        return pltpu.make_async_remote_copy(
+            src_ref=xs.at[source],
+            dst_ref=xs.at[target],
+            send_sem=ag_send.at[index],
+            recv_sem=ag_recv.at[index],
+            device_id=peer,
+            device_id_type=MESH,
+        )
+
+    z_hop = [None] + [hop(j - 1, 0, j, z_peers[j]) for j in (1, 2, 3)]
+    y_hop = [hop(3 + j, j, 4 + j, y_peer) for j in range(4)]
+    c_hop = [hop(7 + s, s, 8 + s, core_peer) for s in range(8)]
+    y_hop[0].start()
+    z_hop[3].start()
+    z_hop[2].start()
+    z_hop[1].start()
+    c_hop[0].start()
+
+    own = table[:, 0:1] * down_bias_ref[0:1, :]
+    for k in range(1, EXPERTS):
+        own += table[:, k : k + 1] * down_bias_ref[k : k + 1, :]
+    base[...] = own
+    bias_t[...] = jnp.transpose(bias_ref[...])
+
+    for j in (1, 2, 3):
+        z_hop[j].wait_recv()
+        y_hop[j].start()
+        c_hop[j].start()
+        y_hop[j - 1].wait_recv()
+        c_hop[4 + j - 1].start()
+    y_hop[3].wait_recv()
+    c_hop[7].start()
+    for s in range(8):
+        c_hop[s].wait_recv()
+
+    everything = xs[...].reshape(16 * rows, wide)
+    xt[...] = jnp.transpose(everything[:, :model])
+    spread = everything[:, wide - 128 :]
+    row_at = lax.broadcasted_iota(jnp.int32, (16, 128), 0)
+    lane_at = lax.broadcasted_iota(jnp.int32, (16, 128), 1)
+    select = jnp.where(
+        (lane_at % EXPERTS == row_at + e * count) & (lane_at < 2 * EXPERTS) & (row_at < count), 1.0, 0.0
+    ).astype(jnp.bfloat16)
+    shares = lax.dot_general(
+        select, spread, (((1,), (1,)), ((), ())), preferred_element_type=jnp.float32
+    )
+
+    for l in range(count):
+        loads[l].wait()
+        gate = jnp.dot(wg[l, 0], xt[...], preferred_element_type=jnp.float32)
+        gate = gate + bias_t[:, 2 * l : 2 * l + 1]
+        up = jnp.dot(wg[l, 1], xt[...], preferred_element_type=jnp.float32)
+        up = up + bias_t[:, 2 * l + 1 : 2 * l + 2]
+        hidden = gate * jax.nn.sigmoid(1.702 * gate) * (up + 1.0) * shares[l : l + 1, :]
+        ht[l * half_width : (l + 1) * half_width, :] = hidden.astype(jnp.bfloat16)
+    hid[...] = jnp.transpose(ht[...])
+    for l in range(count):
+        loads[count + l].wait()
+
+    starts = [sum(widths[:c]) for c in range(chunks)]
+
+    def rs_hop(c, index, source, target, peer):
+        return pltpu.make_async_remote_copy(
+            src_ref=source,
+            dst_ref=target,
+            send_sem=rs_send.at[c * 5 + index],
+            recv_sem=rs_recv.at[c * 5 + index],
+            device_id=peer,
+            device_id_type=MESH,
+        )
+
+    hop1 = [rs_hop(c, 0, send1[c], recv1[c], core_peer) for c in range(chunks)]
+    hop2 = [rs_hop(c, 1, send2[c], recv2[c], y_peer) for c in range(chunks)]
+    hop3 = [
+        [
+            rs_hop(c, 1 + j, send3[c].at[j - 1], recv3[c].at[j - 1], z_peers[j])
+            for j in (1, 2, 3)
+        ]
+        for c in range(chunks)
+    ]
+
+    def stage1(c):
+        at, width = starts[c], widths[c]
+        part = jnp.dot(
+            hid[...], wd[:, at : at + width], preferred_element_type=jnp.float32
+        )
+        send1[c][...] = part[8 * rows :].astype(jnp.bfloat16)
+        hop1[c].start()
+        keep[:, at : at + width] = part[: 8 * rows]
+
+    def stage2(c):
+        at, width = starts[c], widths[c]
+        hop1[c].wait_recv()
+        send2[c][...] = (
+            keep[4 * rows :, at : at + width] + recv1[c][4 * rows :].astype(jnp.float32)
+        ).astype(jnp.bfloat16)
+        hop2[c].start()
+        keep[: 4 * rows, at : at + width] = keep[: 4 * rows, at : at + width] + recv1[c][
+            : 4 * rows
+        ].astype(jnp.float32)
+
+    def stage3(c):
+        at, width = starts[c], widths[c]
+        hop2[c].wait_recv()
+        for j in (3, 2, 1):
+            band = slice(j * rows, (j + 1) * rows)
+            send3[c][j - 1] = (
+                keep[band, at : at + width] + recv2[c][band].astype(jnp.float32)
+            ).astype(jnp.bfloat16)
+            hop3[c][j - 1].start()
+        keep[:rows, at : at + width] = keep[:rows, at : at + width] + recv2[c][:rows].astype(
+            jnp.float32
+        )
+
+    def stage4(c):
+        at, width = starts[c], widths[c]
+        total = keep[:rows, at : at + width] + base[:, at : at + width]
+        for j in (1, 2, 3):
+            hop3[c][j - 1].wait_recv()
+            total += recv3[c][j - 1].astype(jnp.float32)
+        out_ref[:, at : at + width] = total.astype(jnp.bfloat16)
+
+    for step in range(chunks + 3):
+        for lag, stage in enumerate((stage1, stage2, stage3, stage4)):
+            if 0 <= step - lag < chunks:
+                stage(step - lag)
+
+    for copy in z_hop[1:] + y_hop + c_hop + hop1 + hop2 + sum(hop3, []):
+        copy.wait_send()
+
+
+def fused_local(tokens, routes, route_weights, w_gate_up, bias_gate_up, w_down, down_bias):
+    rows, model = tokens.shape
+    count, _, _, half_width = w_gate_up.shape
+    widths = []
+    while sum(widths) < model:
+        widths.append(min(768, model - sum(widths)))
+    wide = -(-model // 128) * 128 + 128
+    total = 16 * rows
+    bf16, f32 = jnp.bfloat16, jnp.float32
+    scratch = [
+        pltpu.VMEM((count, 2, half_width, model), bf16),
+        pltpu.VMEM((count * half_width, model), bf16),
+        pltpu.VMEM((16, rows, wide), bf16),
+        pltpu.VMEM((model, total), bf16),
+        pltpu.VMEM((count * half_width, total), bf16),
+        pltpu.VMEM((total, count * half_width), bf16),
+        pltpu.VMEM((half_width, 2 * count), f32),
+        pltpu.VMEM((8 * rows, model), f32),
+        pltpu.VMEM((rows, model), f32),
+        pltpu.SemaphoreType.DMA((15,)),
+        pltpu.SemaphoreType.DMA((15,)),
+        pltpu.SemaphoreType.DMA((5 * len(widths),)),
+        pltpu.SemaphoreType.DMA((5 * len(widths),)),
+        pltpu.SemaphoreType.DMA((2 * count,)),
+    ]
+    for shape in ((8 * rows,), (4 * rows,), (3, rows)):
+        for _ in range(2):
+            scratch += [pltpu.VMEM(shape + (w,), bf16) for w in widths]
+    in_vmem = pl.BlockSpec(memory_space=pltpu.VMEM)
+    return pl.pallas_call(
+        functools.partial(fused, tuple(widths)),
+        out_shape=jax.ShapeDtypeStruct((rows, model), bf16),
+        in_specs=[in_vmem] * 5 + [pl.BlockSpec(memory_space=pl.ANY)] * 2,
+        out_specs=in_vmem,
+        scratch_shapes=scratch,
+        compiler_params=pltpu.CompilerParams(
+            collective_id=0, has_side_effects=True, vmem_limit_bytes=63 * 1024 * 1024
+        ),
+        cost_estimate=pl.CostEstimate(
+            flops=6 * total * count * half_width * model,
+            bytes_accessed=6 * count * half_width * model,
+            transcendentals=total * count * half_width,
+        ),
+    )(
+        tokens,
+        jnp.transpose(routes),
+        jnp.transpose(route_weights),
+        bias_gate_up.reshape(2 * count, half_width),
+        down_bias,
+        jnp.transpose(w_gate_up, (0, 2, 3, 1)),
+        w_down,
+    )
+
+
 def solution(mesh):
+    small = mesh.shape["expert"] == 4 and mesh.shape["tensor"] == 4
     return jax.shard_map(
-        local,
+        fused_local if small else local,
         mesh=mesh,
         in_specs=(
             P(("groups", "expert", "tensor"), None),

time: 257 us -> 57.2 us (0.22)
  waiting for transfers between devices: 187 us -> 0 us
  Pallas kernels: 0 us -> 54.1 us
  matrix products: 30.3 us -> 0 us
  blocking collectives: 15.3 us -> 0 us
  between operations: 14.2 us -> 0.01 us
  starting transfers between devices: 3.53 us -> 0 us
    unnamed x3 -> x0, waiting for transfers between devices: 114 us -> none
    all_gather x1 -> x0, waiting for transfers between devices: 61.6 us -> none  [local(): lax.all_gather(received, 'tensor', axis=0, tiled=True)]
    pallas_call x0 -> x1, Pallas kernels: none -> 54.1 us  [fused_local(): pl.pallas_call(functools.partial(fused, tuple(widths)), out_shape=jax.Sha...]
    dot_general x4 -> x0, matrix products: 30.3 us -> none  [the longest x1 17.5 us: local(): jnp.einsum('...lcd,ldf->...lcf', lax.all_gather(received, 'tensor', axis=...]
    all_to_all x1 -> x0, blocking collectives: 15.3 us -> none  [local(): lax.all_to_all(outgoing, 'expert', split_axis=0, concat_axis=0, tiled=True)]
    all_to_all x1 -> x0, waiting for transfers between devices: 11.2 us -> none  [local(): lax.all_to_all(result, 'expert', split_axis=0, concat_axis=0, tiled=True)]
    all_to_all x1 -> x0, starting transfers between devices: 3.49 us -> none  [local(): lax.all_to_all(result, 'expert', split_axis=0, concat_axis=0, tiled=True)]
  transfers between devices with their start and end apart: 3 -> 0, of which waited for: 3 -> 0; matrix products, arithmetic and copies ran while one was open for 0% -> 0% of each run, Pallas kernels for 0% -> 0%
where the time goes in v1:
time: 57.2 us; the launch traced here: 57 us
  Pallas kernels  54.1 us (95%)
  local copies, waits for them, and re-layouts  2.9 us (5%)
    pallas_call x1, Pallas kernels, fused_local(): pl.pallas_call(functools.partial(fused, tuple(widths)), out_shape=jax.Sha...  54.1 us
    unnamed x1, local copies, waits for them, and re-layouts  1.54 us
    reshape x1, local copies, waits for them, and re-layouts, fused_local(): bias_gate_up.reshape(2 * count, half_width)  1.36 us

profile of v1, /device:TPU:0, one launch (start us, length us, event | category | flops | bytes accessed | tf_op | source)
XLA Modules:
  0.0 57.0 jit_solution(10502424395341186790)
XLA Ops:
  0.0 1.4 %reshape.3.bias_ref = f32[8,720]{1,0:T(8,128)} reshape(f32[4,2,720]{2,1,0:T(2,128)} %param.11) | data formatting | bytes 46080 | tf_op jit(solution)/shard_map/reshape | solution.py:302
  1.4 54.1 %shard_map.73 = bf16[16,2880]{1,0:T(8,128)(2,1)} custom-call(bf16[16,2880]{1,0:T(8,128)(2,1)} %tok_ref.1, s32[4,16]{1,0:T(4,128)} %bitcast.4, f32[4,16]{1,0:T(4,128)} %bitcast.5, f32[8,720]{1,0:T(8,128)} %reshape.3.bias_ref, f32[16,2880]{1,0:T(8,128)} %down_bias_ref.1, bf16[4,2,720,2880]{3,2,1,0:T(8,128)(2,1)} %bitcast.3, bf16[4,720,2880]{2,1,0:T(8,128)(2,1)} %wd_hbm.1), custom_call_target="tpu_custom_call" | custom-call | flops 12740198400 | bytes 49766400 | tf_op jit(solution)/shard_map/pallas_call | solution.py:284
  55.5 1.5 %copy.9 = bf16[16,2880]{1,0:T(8,128)(2,1)} copy(bf16[16,2880]{1,0:T(8,128)(2,1)} %shard_map.73) | data formatting | bytes 184320

commit v2 on v1

--- a/solution.py
+++ b/solution.py
@@ -68,23 +68,18 @@
 
 
 def fused(widths, tok_ref, route_ref, weight_ref, bias_ref, down_bias_ref, wg_hbm, wd_hbm, out_ref, *scratch):
-    (wg, wd, xs, xt, ht, hid, bias_t, keep, base, ag_send, ag_recv, rs_send, rs_recv, w_sem) = scratch[:14]
+    (wg, wd, xa, xb, xta, xtb, acc, hid, bias_t, keep, base, ag_send, ag_recv, rs_send, rs_recv, w_sem) = scratch[:16]
     chunks = len(widths)
     send1, recv1, send2, recv2, send3, recv3 = (
-        scratch[14 + i * chunks : 14 + (i + 1) * chunks] for i in range(6)
+        scratch[16 + i * chunks : 16 + (i + 1) * chunks] for i in range(6)
     )
     count, _, half_width, model = wg_hbm.shape
     rows = tok_ref.shape[0]
     g, e, t = lax.axis_index("groups"), lax.axis_index("expert"), lax.axis_index("tensor")
     core_peer = (g, e + 1 - 2 * (e % 2), t)
     y_peer = (g, (e + 2) % 4, t)
-    z_peers = (
-        None,
-        (g, e, t + 1 - 2 * (t % 2)),
-        (g, e, (t + 2) % 4),
-        (g, e, 3 - t),
-    )
-    partners = (core_peer, y_peer, z_peers[1], z_peers[2], z_peers[3])
+    z_near, z_far = (g, e, t + 1 - 2 * (t % 2)), (g, e, (t + 2) % 4)
+    partners = (core_peer, y_peer, z_near, z_far)
 
     barrier = pltpu.get_barrier_semaphore()
     for partner in partners:
@@ -114,53 +109,101 @@
     high = table.astype(jnp.bfloat16).astype(jnp.float32)
     lane = lax.broadcasted_iota(jnp.int32, (rows, 128), 1)
     coded = jnp.where(lane < EXPERTS, high, jnp.where(lane < 2 * EXPERTS, table - high, 0.0))
-    wide = xs.shape[2]
-    xs[0, :, :model] = tok_ref[...]
-    xs[0, :, wide - 128 :] = coded.astype(jnp.bfloat16)
+    xs = (xa, xb)
+    cut, rest = xa.shape[2], model - xa.shape[2]
+    spare = xb.shape[2] - rest
+    xa[0] = tok_ref[:, :cut]
+    xb[0] = jnp.concatenate([tok_ref[:, cut:], coded[:, :spare].astype(jnp.bfloat16)], axis=1)
 
     pl.semaphore_wait(barrier, len(partners))
 
-    def hop(index, source, target, peer):
+    def hop(half, index, source, target, peer):
         return pltpu.make_async_remote_copy(
-            src_ref=xs.at[source],
-            dst_ref=xs.at[target],
-            send_sem=ag_send.at[index],
-            recv_sem=ag_recv.at[index],
+            src_ref=xs[half].at[source],
+            dst_ref=xs[half].at[target],
+            send_sem=ag_send.at[half * 14 + index],
+            recv_sem=ag_recv.at[half * 14 + index],
             device_id=peer,
             device_id_type=MESH,
         )
 
-    z_hop = [None] + [hop(j - 1, 0, j, z_peers[j]) for j in (1, 2, 3)]
-    y_hop = [hop(3 + j, j, 4 + j, y_peer) for j in range(4)]
-    c_hop = [hop(7 + s, s, 8 + s, core_peer) for s in range(8)]
-    y_hop[0].start()
-    z_hop[3].start()
-    z_hop[2].start()
-    z_hop[1].start()
-    c_hop[0].start()
+    z_hop = [
+        [None, hop(h, 0, 0, 1, z_near), hop(h, 1, 0, 2, z_far), hop(h, 2, 2, 3, z_near)]
+        for h in (0, 1)
+    ]
+    y_hop = [[hop(h, 3 + j, j, 4 + j, y_peer) for j in range(4)] for h in (0, 1)]
+    c_hop = [[hop(h, 7 + s, s, 8 + s, core_peer) for s in range(7)] for h in (0, 1)]
+    for h in (0, 1):
+        c_hop[h].append(
+            pltpu.make_async_remote_copy(
+                src_ref=xs[h].at[7],
+                dst_ref=xs[h].at[15],
+                send_sem=ag_send.at[28 + h],
+                recv_sem=ag_recv.at[28 + h],
+                device_id=core_peer,
+                device_id_type=MESH,
+            )
+        )
+    for h in (0, 1):
+        y_hop[h][0].start()
+        z_hop[h][1].start()
+        z_hop[h][2].start()
+        c_hop[h][0].start()
 
     own = table[:, 0:1] * down_bias_ref[0:1, :]
     for k in range(1, EXPERTS):
         own += table[:, k : k + 1] * down_bias_ref[k : k + 1, :]
     base[...] = own
-    bias_t[...] = jnp.transpose(bias_ref[...])
-
-    for j in (1, 2, 3):
-        z_hop[j].wait_recv()
-        y_hop[j].start()
-        c_hop[j].start()
-        y_hop[j - 1].wait_recv()
-        c_hop[4 + j - 1].start()
-    y_hop[3].wait_recv()
-    c_hop[7].start()
-    for s in range(8):
-        c_hop[s].wait_recv()
-
-    everything = xs[...].reshape(16 * rows, wide)
-    xt[...] = jnp.transpose(everything[:, :model])
-    spread = everything[:, wide - 128 :]
-    row_at = lax.broadcasted_iota(jnp.int32, (16, 128), 0)
-    lane_at = lax.broadcasted_iota(jnp.int32, (16, 128), 1)
+    bias_t[...] = jnp.transpose(jnp.concatenate([bias_ref[l] for l in range(count)], axis=0))
+
+    def z_in(h, j):
+        z_hop[h][j].wait_recv()
+        if j == 2:
+            z_hop[h][3].start()
+        y_hop[h][j].start()
+        c_hop[h][j].start()
+
+    def y_in(h, j):
+        y_hop[h][j].wait_recv()
+        c_hop[h][4 + j].start()
+
+    def all_in(h):
+        for s in range(8):
+            c_hop[h][s].wait_recv()
+
+    z_in(0, 1)
+    y_in(0, 0)
+    z_in(0, 2)
+    y_in(1, 0)
+    z_in(1, 1)
+    y_in(0, 1)
+    z_in(1, 2)
+    z_in(0, 3)
+    y_in(0, 2)
+    y_in(1, 1)
+    z_in(1, 3)
+    y_in(1, 2)
+    y_in(0, 3)
+    all_in(0)
+    xta[...] = jnp.transpose(xa[...].reshape(16 * rows, cut))
+
+    def first_half(l, part):
+        return jnp.dot(wg[l, part, :, :cut], xta[...], preferred_element_type=jnp.float32)
+
+    early = acc.shape[0]
+    for l in range(early):
+        loads[l].wait()
+        for part in (0, 1):
+            acc[l, part] = first_half(l, part)
+        if l == 0:
+            y_in(1, 3)
+    all_in(1)
+
+    everything = xb[...].reshape(16 * rows, rest + spare)
+    xtb[...] = jnp.transpose(everything[:, :rest])
+    spread = everything[:, rest:]
+    row_at = lax.broadcasted_iota(jnp.int32, (16, spare), 0)
+    lane_at = lax.broadcasted_iota(jnp.int32, (16, spare), 1)
     select = jnp.where(
         (lane_at % EXPERTS == row_at + e * count) & (lane_at < 2 * EXPERTS) & (row_at < count), 1.0, 0.0
     ).astype(jnp.bfloat16)
@@ -169,14 +212,18 @@
     )
 
     for l in range(count):
-        loads[l].wait()
-        gate = jnp.dot(wg[l, 0], xt[...], preferred_element_type=jnp.float32)
-        gate = gate + bias_t[:, 2 * l : 2 * l + 1]
-        up = jnp.dot(wg[l, 1], xt[...], preferred_element_type=jnp.float32)
-        up = up + bias_t[:, 2 * l + 1 : 2 * l + 2]
+        if l >= early:
+            loads[l].wait()
+        gate, up = (
+            (acc[l, part] if l < early else first_half(l, part))
+            + jnp.dot(wg[l, part, :, cut:], xtb[...], preferred_element_type=jnp.float32)
+            + bias_t[:, 2 * l + part : 2 * l + part + 1]
+            for part in (0, 1)
+        )
         hidden = gate * jax.nn.sigmoid(1.702 * gate) * (up + 1.0) * shares[l : l + 1, :]
-        ht[l * half_width : (l + 1) * half_width, :] = hidden.astype(jnp.bfloat16)
-    hid[...] = jnp.transpose(ht[...])
+        hid[:, l * half_width : (l + 1) * half_width] = jnp.transpose(
+            hidden.astype(jnp.bfloat16)
+        )
     for l in range(count):
         loads[count + l].wait()
 
@@ -196,7 +243,7 @@
     hop2 = [rs_hop(c, 1, send2[c], recv2[c], y_peer) for c in range(chunks)]
     hop3 = [
         [
-            rs_hop(c, 1 + j, send3[c].at[j - 1], recv3[c].at[j - 1], z_peers[j])
+            rs_hop(c, 1 + j, send3[c].at[j - 1], recv3[c].at[j - 1], z_far if j == 2 else z_near)
             for j in (1, 2, 3)
         ]
         for c in range(chunks)
@@ -225,30 +272,45 @@
     def stage3(c):
         at, width = starts[c], widths[c]
         hop2[c].wait_recv()
-        for j in (3, 2, 1):
+        for j in (3, 1):
             band = slice(j * rows, (j + 1) * rows)
             send3[c][j - 1] = (
                 keep[band, at : at + width] + recv2[c][band].astype(jnp.float32)
             ).astype(jnp.bfloat16)
             hop3[c][j - 1].start()
-        keep[:rows, at : at + width] = keep[:rows, at : at + width] + recv2[c][:rows].astype(
-            jnp.float32
-        )
 
     def stage4(c):
         at, width = starts[c], widths[c]
+        band = slice(2 * rows, 3 * rows)
+        both = keep[band, at : at + width] + recv2[c][band].astype(jnp.float32)
+        hop3[c][2].wait_recv()
+        send3[c][1] = (both + recv3[c][2].astype(jnp.float32)).astype(jnp.bfloat16)
+        hop3[c][1].start()
+
+    def stage5(c):
+        at, width = starts[c], widths[c]
         total = keep[:rows, at : at + width] + base[:, at : at + width]
-        for j in (1, 2, 3):
+        total += recv2[c][:rows].astype(jnp.float32)
+        for j in (1, 2):
             hop3[c][j - 1].wait_recv()
             total += recv3[c][j - 1].astype(jnp.float32)
         out_ref[:, at : at + width] = total.astype(jnp.bfloat16)
 
-    for step in range(chunks + 3):
-        for lag, stage in enumerate((stage1, stage2, stage3, stage4)):
-            if 0 <= step - lag < chunks:
-                stage(step - lag)
-
-    for copy in z_hop[1:] + y_hop + c_hop + hop1 + hop2 + sum(hop3, []):
+    for step in range(chunks + 1):
+        if step < chunks:
+            stage1(step)
+        if step >= 1:
+            stage2(step - 1)
+    for step in range(chunks + 2):
+        if step < chunks:
+            stage3(step)
+        if step >= 2:
+            stage4(step - 2)
+    for c in range(chunks):
+        stage5(c)
+
+    ag_hops = [copy for h in (0, 1) for copy in z_hop[h][1:] + y_hop[h] + c_hop[h]]
+    for copy in ag_hops + hop1 + hop2 + sum(hop3, []):
         copy.wait_send()
 
 
@@ -257,22 +319,25 @@
     count, _, _, half_width = w_gate_up.shape
     widths = []
     while sum(widths) < model:
-        widths.append(min(768, model - sum(widths)))
-    wide = -(-model // 128) * 128 + 128
+        widths.append(min(512, model - sum(widths)))
+    wide = -(-(model + 2 * EXPERTS) // 128) * 128
+    cut = wide // 512 * 256 + 256
     total = 16 * rows
     bf16, f32 = jnp.bfloat16, jnp.float32
     scratch = [
         pltpu.VMEM((count, 2, half_width, model), bf16),
         pltpu.VMEM((count * half_width, model), bf16),
-        pltpu.VMEM((16, rows, wide), bf16),
-        pltpu.VMEM((model, total), bf16),
-        pltpu.VMEM((count * half_width, total), bf16),
+        pltpu.VMEM((16, rows, cut), bf16),
+        pltpu.VMEM((16, rows, wide - cut), bf16),
+        pltpu.VMEM((cut, total), bf16),
+        pltpu.VMEM((model - cut, total), bf16),
+        pltpu.VMEM((2, 2, half_width, total), f32),
         pltpu.VMEM((total, count * half_width), bf16),
         pltpu.VMEM((half_width, 2 * count), f32),
         pltpu.VMEM((8 * rows, model), f32),
         pltpu.VMEM((rows, model), f32),
-        pltpu.SemaphoreType.DMA((15,)),
-        pltpu.SemaphoreType.DMA((15,)),
+        pltpu.SemaphoreType.DMA((30,)),
+        pltpu.SemaphoreType.DMA((30,)),
         pltpu.SemaphoreType.DMA((5 * len(widths),)),
         pltpu.SemaphoreType.DMA((5 * len(widths),)),
         pltpu.SemaphoreType.DMA((2 * count,)),
@@ -299,7 +364,7 @@
         tokens,
         jnp.transpose(routes),
         jnp.transpose(route_weights),
-        bias_gate_up.reshape(2 * count, half_width),
+        bias_gate_up,
         down_bias,
         jnp.transpose(w_gate_up, (0, 2, 3, 1)),
         w_down,

time: 57.2 us -> 50.7 us (0.89)
  Pallas kernels: 54.1 us -> 49 us
  local copies, waits for them, and re-layouts: 2.9 us -> 1.54 us
    pallas_call x1, Pallas kernels: 54.1 us -> 49 us  [fused_local(): pl.pallas_call(functools.partial(fused, tuple(widths)), out_shape=jax.Sha...]
    reshape x1 -> x0, local copies, waits for them, and re-layouts: 1.36 us -> none  [fused_local(): bias_gate_up.reshape(2 * count, half_width)]
where the time goes in v2:
time: 50.7 us; the launch traced here: 50.6 us
  Pallas kernels  49 us (97%)
  local copies, waits for them, and re-layouts  1.54 us (3%)
    pallas_call x1, Pallas kernels, fused_local(): pl.pallas_call(functools.partial(fused, tuple(widths)), out_shape=jax.Sha...  49 us
    unnamed x1, local copies, waits for them, and re-layouts  1.54 us

profile of v2, /device:TPU:0, one launch (start us, length us, event | category | flops | bytes accessed | tf_op | source)
XLA Modules:
  0.0 50.6 jit_solution(11570345232465910568)
XLA Ops:
  0.0 49.0 %shard_map.73 = bf16[16,2880]{1,0:T(8,128)(2,1)} custom-call(bf16[16,2880]{1,0:T(8,128)(2,1)} %tok_ref.1, s32[4,16]{1,0:T(4,128)} %bitcast.4, f32[4,16]{1,0:T(4,128)} %bitcast.5, f32[4,2,720]{2,1,0:T(2,128)} %bias_ref.1, f32[16,2880]{1,0:T(8,128)} %down_bias_ref.1, bf16[4,2,720,2880]{3,2,1,0:T(8,128)(2,1)} %bitcast.3, bf16[4,720,2880]{2,1,0:T(8,128)(2,1)} %wd_hbm.1), custom_call_target="tpu_custom_call" | custom-call | flops 12740198400 | bytes 49766400 | tf_op jit(solution)/shard_map/pallas_call | solution.py:349
  49.0 1.5 %copy.9 = bf16[16,2880]{1,0:T(8,128)(2,1)} copy(bf16[16,2880]{1,0:T(8,128)(2,1)} %shard_map.73) | data formatting | bytes 184320
